TPU v7x, 32 devices: a whole 2x2x4 slice. The times are simulated.
32 devices in a mesh: groups: 2 (over x), ctx: 16 (over z, y, core).
Axes of the slice: x: 2, y: 2, z: 4, core: 2. Of those that a mesh axis runs over, the one named last changes fastest.
Arguments:
- hidden: bfloat16 [16384, 1024], P(('groups', 'ctx')), parts along dimension 0, may hold values from -6 to 6
- query_weight: bfloat16 [1024, 1024], replicated, may hold values from -0.1875 to 0.1875
- key_weight: bfloat16 [1024, 1024], replicated, may hold values from -0.1875 to 0.1875
- value_weight: bfloat16 [1024, 1024], replicated, may hold values from -0.1875 to 0.1875
- output_weight: bfloat16 [1024, 1024], replicated, may hold values from -0.1875 to 0.1875
- decay_log: float32 [16384, 8], P(('groups', 'ctx')), parts along dimension 0, may hold values from -1 to 0, as said below
- doc_starts: int32 [8], P('groups'), parts along dimension 0, may hold values from 0 to 8128, as said below
Outputs:
- mixed: bfloat16 [16384, 1024], P(('groups', 'ctx')), parts along dimension 0
There are 2 independent parts, one for each index of `groups`. A program takes and returns all parts, laid end to end along the dimension named above; an argument that names none is the same for every part. Nothing has to cross between parts.
Inputs may be any that keep to these rules, and one draw needn't show every extreme that they name: Every entry of decay_log is negative. doc_starts is non-decreasing, its first entry is 0, its last entry is 8128, and every entry is a multiple of 64; a repeated entry marks an empty document.
All inputs are finite; a program needn't handle non-finite values.
Results may differ from a plain program's by a relative error of at most 0.0069.
Values sent between devices are 32-bit elements; how exact they have to be, the bound alone decides.
A program may use at most 192 MiB of HBM per device.

v0:
```python
import jax
import jax.numpy as jnp
from jax import lax
from jax.sharding import PartitionSpec as P

D = 1024
HEAD_COUNT = 8
HEAD = 128
BLOCK = 64


def prefix(part, axis, combine, identity):
    place = lax.axis_index(axis)
    gathered = jax.tree.map(lambda a: lax.all_gather(a, axis), part)
    state = jax.tree.map(lambda a, e: jnp.zeros_like(a) + jnp.asarray(e, a.dtype), part, identity)

    def one(turn, state):
        return combine(
            state, jax.tree.map(lambda a: lax.dynamic_index_in_dim(a, turn, 0, False), gathered)
        )

    return lax.fori_loop(0, place, one, state)


def project(hidden, weight, shape):
    return (
        jnp.dot(hidden, weight, preferred_element_type=jnp.float32)
        .astype(jnp.bfloat16)
        .reshape(shape)
    )


def combine_states(first_part, second_part):
    first_decay, first_state = first_part
    second_decay, second_state = second_part
    return (first_decay * second_decay, second_state + second_decay[:, None, None] * first_state)


def body(hidden, query_weight, key_weight, value_weight, output_weight, decay_log, doc_starts):
    tok_rows = hidden.shape[0]
    blocks = tok_rows // BLOCK
    device = lax.axis_index("ctx")
    shape_four = (blocks, BLOCK, HEAD_COUNT, HEAD)
    queries = project(hidden, query_weight, shape_four)
    key_rows = project(hidden, key_weight, shape_four)
    value_rows = project(hidden, value_weight, shape_four)
    cumulative = jnp.cumsum(decay_log.reshape(blocks, BLOCK, HEAD_COUNT), axis=1)
    positions = device * tok_rows + jnp.arange(blocks, dtype=jnp.int32) * BLOCK
    resets = jnp.any(positions[:, None] == doc_starts[None, :], axis=1)
    keeps = jnp.where(resets, 0.0, 1.0).astype(jnp.float32)
    lower_mask = jnp.arange(BLOCK)[:, None] >= jnp.arange(BLOCK)[None, :]
    scores = jnp.einsum("bjhd,bihd->bhji", queries, key_rows, preferred_element_type=jnp.float32)
    cum_heads = jnp.swapaxes(cumulative, 1, 2)
    gap_matrix = cum_heads[:, :, :, None] - cum_heads[:, :, None, :]
    weights = (jnp.where(lower_mask, jnp.exp(gap_matrix), 0.0) * scores).astype(jnp.bfloat16)
    intra_term = jnp.einsum(
        "bhji,bihd->bjhd", weights, value_rows, preferred_element_type=jnp.float32
    )
    block_tail = cumulative[:, -1, :]
    scaled = key_rows.astype(jnp.float32) * jnp.exp(block_tail[:, None, :] - cumulative)[..., None]
    block_terms = jnp.einsum(
        "bihd,bihe->bhde", scaled, value_rows.astype(jnp.float32), precision=lax.Precision.HIGHEST
    )
    block_decay = jnp.exp(block_tail)

    def carry_block(carry, inputs):
        state_now, factor_now = carry
        block_term, decay_now, keep_flag = inputs
        state_in = state_now * keep_flag
        factor_in = factor_now * keep_flag
        return (
            (state_in * decay_now[:, None, None] + block_term, factor_in * decay_now),
            (state_in, factor_in),
        )

    start_state = jnp.zeros((HEAD_COUNT, HEAD, HEAD), jnp.float32)
    start_factor = jnp.ones((HEAD_COUNT,), jnp.float32)
    (local_end, span_decay), (entering, factors) = lax.scan(
        carry_block, (start_state, start_factor), (block_terms, block_decay, keeps)
    )
    query_wide = queries.astype(jnp.float32)
    growth = jnp.exp(cumulative)[..., None]
    inter_term = (
        jnp.einsum("bjhd,bhde->bjhe", query_wide, entering, precision=lax.Precision.HIGHEST)
        * growth
    )
    identity = (jnp.ones_like(span_decay), jnp.zeros_like(local_end))
    incoming = prefix((span_decay, local_end), "ctx", combine_states, identity)[1]
    carried = jnp.einsum(
        "bjhd,hde->bjhe", query_wide, incoming, precision=lax.Precision.HIGHEST
    ) * (growth * factors[:, None, :, None])
    attended = intra_term + inter_term + carried
    normed = attended * lax.rsqrt(jnp.mean(attended * attended, axis=3, keepdims=True) + 1e-06)
    normed = normed.astype(jnp.bfloat16).reshape(tok_rows, D)
    return jnp.dot(normed, output_weight, preferred_element_type=jnp.float32).astype(jnp.bfloat16)


def solution(mesh):
    in_specs = (
        P(("groups", "ctx"), None),
        P(),
        P(),
        P(),
        P(),
        P(("groups", "ctx"), None),
        P("groups"),
    )
    out_specs = P(("groups", "ctx"), None)
    return jax.shard_map(body, mesh=mesh, in_specs=in_specs, out_specs=out_specs, check_vma=False)
```

profile of v0, /device:TPU:27, one launch (start us, length us, event | category | flops | bytes accessed | tf_op | source)
XLA Modules:
  0.0 171.3 jit_solution(11579919578728413585)
XLA Ops:
  6.5 0.9 reshape.50
  7.6 6.3 %fusion.35 = f32[8,64,8]{2,0,1:T(8,128)S(1)} fusion(f32[8,64,8]{2,0,1:T(8,128)S(1)} %copy.47), kind=kOutput, calls=%fused_computation.56 | output fusion | flops 258048 | bytes 32768 | tf_op jit(solution)/shard_map/jit(cumsum)/reduce_window_sum | solution.py:47
  14.2 2.6 %fusion.11 = bf16[64,8,8,128]{3,1,2,0:T(8,128)(2,1)S(1)} fusion(bf16[512,1024]{1,0:T(8,128)(2,1)} %param.11, bf16[1024,1024]{1,0:T(8,128)(2,1)S(1)} %copy-done), kind=kOutput, calls=%fused_computation.27 | convolution fusion | flops 1074266112 | bytes 4194304 | tf_op jit(solution)/shard_map/dot_general | solution.py:27
  16.9 1.3 copy.62
  18.2 1.3 fusion.9
  19.4 1.3 copy.63
  20.8 7.5 %fusion.6 = f32[8,8,128,128]{3,2,1,0:T(8,128)} fusion(f32[8,64,8]{1,2,0:T(8,128)S(1)} %copy.54, bf16[8,64,8,128]{3,2,1,0:T(8,128)(2,1)} %bitcast.82, bf16[8,64,8,128]{3,2,1,0:T(8,128)(2,1)} %bitcast.80), kind=kOutput, calls=%fused_computation.17 | convolution fusion | flops 806354944 | bytes 6307840 | tf_op jit(solution)/shard_map/bihd,bihe->bhde/dot_general | solution.py:61
  28.3 36.4 %while.30 = (s32[]{:T(128)}, f32[8,128,128]{2,1,0:T(8,128)S(1)}, f32[8]{0:T(128)S(1)}, f32[8,8,128,128]{3,2,1,0:T(8,128)}, f32[8,8]{1,0:T(8,128)S(1)}, /*index=5...) while((s32[]{:T(128)}, f32[8,128,128]{2,1,0:T(8,128)S(1)}, ...), condition=%wide.region_3.4_spmd.clone, body=%wide.region_2.3_spmd.clone.sunk | while | flops 786459 | bytes 2622865 | solution.py:78
  29.6 1.5 bitcast_dynamic-update-slice_fusion.2
  31.1 1.8 %bitcast_add_fusion.5 = f32[8,128,128]{2,1,0:T(8,128)S(1)} fusion(f32[8,8,128,128]{3,2,1,0:T(8,128)} %get-tuple-element.273, s32[]{:T(128)} %get-tuple-element.256, f32[8,128,128]{2,1,0:T(8,128)S(1)} %get-tuple-element.257, f32[8]{0:T(128)S(1)} %get-tuple-element.243, f32[]{:T(128)} %bitcast.75, pred[]{:T(512)S(6)} %compare.3), kind=kLoop, calls=%fused_computation.3.clone.1 | loop fusion | flops 524288 | bytes 1572905 | tf_op jit(solution)/shard_map/while/body/eval_jaxpr/add | solution.py:72
  34.1 1.5 bitcast_dynamic-update-slice_fusion.2
  35.6 1.8 %bitcast_add_fusion.5 = f32[8,128,128]{2,1,0:T(8,128)S(1)} fusion(f32[8,8,128,128]{3,2,1,0:T(8,128)} %get-tuple-element.273, s32[]{:T(128)} %get-tuple-element.256, f32[8,128,128]{2,1,0:T(8,128)S(1)} %get-tuple-element.257, f32[8]{0:T(128)S(1)} %get-tuple-element.243, f32[]{:T(128)} %bitcast.75, pred[]{:T(512)S(6)} %compare.3), kind=kLoop, calls=%fused_computation.3.clone.1 | loop fusion | flops 524288 | bytes 1572905 | tf_op jit(solution)/shard_map/while/body/eval_jaxpr/add | solution.py:72
  38.7 1.5 bitcast_dynamic-update-slice_fusion.2
  40.2 1.8 %bitcast_add_fusion.5 = f32[8,128,128]{2,1,0:T(8,128)S(1)} fusion(f32[8,8,128,128]{3,2,1,0:T(8,128)} %get-tuple-element.273, s32[]{:T(128)} %get-tuple-element.256, f32[8,128,128]{2,1,0:T(8,128)S(1)} %get-tuple-element.257, f32[8]{0:T(128)S(1)} %get-tuple-element.243, f32[]{:T(128)} %bitcast.75, pred[]{:T(512)S(6)} %compare.3), kind=kLoop, calls=%fused_computation.3.clone.1 | loop fusion | flops 524288 | bytes 1572905 | tf_op jit(solution)/shard_map/while/body/eval_jaxpr/add | solution.py:72
  43.3 1.4 bitcast_dynamic-update-slice_fusion.2
  44.7 1.8 %bitcast_add_fusion.5 = f32[8,128,128]{2,1,0:T(8,128)S(1)} fusion(f32[8,8,128,128]{3,2,1,0:T(8,128)} %get-tuple-element.273, s32[]{:T(128)} %get-tuple-element.256, f32[8,128,128]{2,1,0:T(8,128)S(1)} %get-tuple-element.257, f32[8]{0:T(128)S(1)} %get-tuple-element.243, f32[]{:T(128)} %bitcast.75, pred[]{:T(512)S(6)} %compare.3), kind=kLoop, calls=%fused_computation.3.clone.1 | loop fusion | flops 524288 | bytes 1572905 | tf_op jit(solution)/shard_map/while/body/eval_jaxpr/add | solution.py:72
  47.8 1.5 bitcast_dynamic-update-slice_fusion.2
  49.3 1.8 %bitcast_add_fusion.5 = f32[8,128,128]{2,1,0:T(8,128)S(1)} fusion(f32[8,8,128,128]{3,2,1,0:T(8,128)} %get-tuple-element.273, s32[]{:T(128)} %get-tuple-element.256, f32[8,128,128]{2,1,0:T(8,128)S(1)} %get-tuple-element.257, f32[8]{0:T(128)S(1)} %get-tuple-element.243, f32[]{:T(128)} %bitcast.75, pred[]{:T(512)S(6)} %compare.3), kind=kLoop, calls=%fused_computation.3.clone.1 | loop fusion | flops 524288 | bytes 1572905 | tf_op jit(solution)/shard_map/while/body/eval_jaxpr/add | solution.py:72
  52.3 1.5 bitcast_dynamic-update-slice_fusion.2
  53.8 1.8 %bitcast_add_fusion.5 = f32[8,128,128]{2,1,0:T(8,128)S(1)} fusion(f32[8,8,128,128]{3,2,1,0:T(8,128)} %get-tuple-element.273, s32[]{:T(128)} %get-tuple-element.256, f32[8,128,128]{2,1,0:T(8,128)S(1)} %get-tuple-element.257, f32[8]{0:T(128)S(1)} %get-tuple-element.243, f32[]{:T(128)} %bitcast.75, pred[]{:T(512)S(6)} %compare.3), kind=kLoop, calls=%fused_computation.3.clone.1 | loop fusion | flops 524288 | bytes 1572905 | tf_op jit(solution)/shard_map/while/body/eval_jaxpr/add | solution.py:72
  56.9 1.4 bitcast_dynamic-update-slice_fusion.2
  58.3 1.8 %bitcast_add_fusion.5 = f32[8,128,128]{2,1,0:T(8,128)S(1)} fusion(f32[8,8,128,128]{3,2,1,0:T(8,128)} %get-tuple-element.273, s32[]{:T(128)} %get-tuple-element.256, f32[8,128,128]{2,1,0:T(8,128)S(1)} %get-tuple-element.257, f32[8]{0:T(128)S(1)} %get-tuple-element.243, f32[]{:T(128)} %bitcast.75, pred[]{:T(512)S(6)} %compare.3), kind=kLoop, calls=%fused_computation.3.clone.1 | loop fusion | flops 524288 | bytes 1572905 | tf_op jit(solution)/shard_map/while/body/eval_jaxpr/add | solution.py:72
  61.4 1.5 bitcast_dynamic-update-slice_fusion.2
  62.9 1.8 %bitcast_add_fusion.5 = f32[8,128,128]{2,1,0:T(8,128)S(1)} fusion(f32[8,8,128,128]{3,2,1,0:T(8,128)} %get-tuple-element.273, s32[]{:T(128)} %get-tuple-element.256, f32[8,128,128]{2,1,0:T(8,128)S(1)} %get-tuple-element.257, f32[8]{0:T(128)S(1)} %get-tuple-element.243, f32[]{:T(128)} %bitcast.75, pred[]{:T(512)S(6)} %compare.3), kind=kLoop, calls=%fused_computation.3.clone.1 | loop fusion | flops 524288 | bytes 1572905 | tf_op jit(solution)/shard_map/while/body/eval_jaxpr/add | solution.py:72
  64.7 0.8 copy-done.1
  67.0 26.4 %all-reduce = f32[128]{0:T(128)S(1)} all-reduce(f32[128]{0:T(128)S(1)} %dynamic-update-slice), channel_id=3, replica_groups=mesh['groups'=2,'ctx'=16] {'ctx'}, use_global_device_ids=true, to_apply=%add | all-reduce | flops 128 | bytes 1024
  93.8 3.2 %fusion.10 = bf16[64,8,8,128]{3,1,2,0:T(8,128)(2,1)S(1)} fusion(bf16[512,1024]{1,0:T(8,128)(2,1)} %param.11, bf16[1024,1024]{1,0:T(8,128)(2,1)} %param.12), kind=kOutput, calls=%fused_computation.26 | convolution fusion | flops 1074266112 | bytes 4194304 | tf_op jit(solution)/shard_map/dot_general | solution.py:27
  97.5 4.1 %fusion.12 = f32[8,8,128,64]{2,3,1,0:T(8,128)} fusion(f32[8,8,64]{2,1,0:T(8,128)S(1)} %copy.48, pred[64,64]{1,0:T(8,128)(4,1)S(1)} %iota_compare_fusion, bf16[8,64,8,128]{3,2,1,0:T(8,128)(2,1)} %bitcast.83, bf16[8,64,8,128]{3,2,1,0:T(8,128)(2,1)} %bitcast.81, bf16[8,64,8,128]{3,2,1,0:T(8,128)(2,1)S(1)} %bitcast.76), kind=kOutput, calls=%fused_computation.28 | convolution fusion | flops 135266304 | bytes 5263360 | tf_op jit(solution)/shard_map/bhji,bihd->bjhd/dot_general | solution.py:56
  101.6 6.0 %fusion.26 = f32[8,8,128,64]{2,3,1,0:T(8,128)} fusion(f32[8,8,128,128]{3,2,1,0:T(8,128)} %get-tuple-element.94, bf16[8,64,8,128]{3,2,1,0:T(8,128)(2,1)S(1)} %bitcast.77), kind=kOutput, calls=%fused_computation.41 | convolution fusion | flops 805306368 | bytes 7340032 | tf_op jit(solution)/shard_map/bjhd,bhde->bjhe/dot_general | solution.py:84
  107.6 32.8 %all-gather.4.cloned.1.call-done = f32[128,128,128]{2,1,0:T(8,128)} async-done(((f32[8,128,128]{2,1,0:T(8,128)}), f32[128,128,128]{2,1,0:T(8,128)}) %all-gather.4.cloned.1.call-update) | async-done | bytes 8388624 | tf_op jit(solution)/shard_map/all_gather | solution.py:14
  140.4 16.1 %while.29 = (s32[]{:T(128)}, f32[8,128,128]{2,1,0:T(8,128)S(1)}, s32[]{:T(128)}, f32[16,8,128,128]{3,2,1,0:T(8,128)}, f32[16,8]{1,0:T(8,128)S(1)}, /*index=5*/s32[]{:T(128)}, s32[]{:T(128)}, s32[]{:T(128)}) while((s32[]{:T(128)}, f32[8,128,128]{2,1,0:T(8,128)S(1)}, s32[]{:T(128)}, f32[16,8,128,128]{3,2,1,0:T(8,128)}, f32[16,8]{1,0:T(8,128)S(1)}, ...), condition=%wide.region_5.6_spmd, body=%wide.region_4.5_spmd.sunk | while | flops 262149 | bytes 1573087 | solution.py:22
  140.5 1.2 bitcast_add_fusion.4
  141.7 1.2 bitcast_add_fusion.4
  143.0 1.2 bitcast_add_fusion.4
  144.2 1.2 bitcast_add_fusion.4
  145.4 1.2 bitcast_add_fusion.4
  146.7 1.2 bitcast_add_fusion.4
  147.9 1.2 bitcast_add_fusion.4
  149.2 1.2 bitcast_add_fusion.4
  150.4 1.2 bitcast_add_fusion.4
  151.6 1.2 bitcast_add_fusion.4
  152.9 1.2 bitcast_add_fusion.4
  154.1 1.2 bitcast_add_fusion.4
  155.3 1.2 bitcast_add_fusion.4
  156.6 4.0 %multiply_reduce_fusion = (f32[8,64,8]{1,2,0:T(8,128)S(1)}, f32[8,64,8,128]{3,1,2,0:T(8,128)S(1)}) fusion(f32[8,64,8]{1,2,0:T(8,128)S(1)} %copy.59, bf16[8,64,8,128]{3,2,1,0:T(8,128)(2,1)} %bitcast.78, f32[8,128,128]{2,1,0:T(8,128)S(1)} %get-tuple-element.97, f32[8,64,8]{1,2,0:T(8,128)S(1)} %copy.57, f32[8,8,128,64]{2,3,1,0:T(8,128)} %fusion.26, ...), kind=kOutput, calls=%fused_computation.16 | convolution fusion | flops 808448000 | bytes 7913472 | tf_op jit(solution)/shard_map/bjhd,hde->bjhe/dot_general | solution.py:89
  160.6 0.7 multiply_convert_fusion
  161.3 0.7 copy.60
  162.2 2.2 %convolution_convert_fusion = bf16[512,1024]{1,0:T(8,128)(2,1)} fusion(bf16[1024,1024]{1,0:T(8,128)(2,1)S(1)} %copy-done.4, bf16[64,8,8,128]{3,2,1,0:T(8,128)(2,1)S(1)} %bitcast.84), kind=kOutput, calls=%fused_computation.21 | convolution fusion | flops 1074266112 | bytes 4194304 | tf_op jit(solution)/shard_map/dot_general | solution.py:95
  (78 shorter events, 12.7 us)
Async XLA Ops:
  6.5 7.7 %copy-start = (bf16[1024,1024]{1,0:T(8,128)(2,1)S(1)}, bf16[1024,1024]{1,0:T(8,128)(2,1)}, u32[]{:S(2)}) copy-start(bf16[1024,1024]{1,0:T(8,128)(2,1)} %param.13) | copy-start | bytes 6291460
  6.5 133.9 %all-gather.4.cloned.1.call-start = ((), (), s32[]{:S(2)}) async-start(), calls=%async_computation | async-start | bytes 8912896 | tf_op jit(solution)/shard_map/all_gather | solution.py:14
  14.2 3.9 %copy-start.3 = (bf16[1024,1024]{1,0:T(8,128)(2,1)S(1)}, bf16[1024,1024]{1,0:T(8,128)(2,1)}, u32[]{:S(2)}) copy-start(bf16[1024,1024]{1,0:T(8,128)(2,1)} %param.14) | copy-start | bytes 6291460
  14.2 3.9 %copy-start.5 = (bf16[512,1024]{1,0:T(8,128)(2,1)S(1)}, bf16[512,1024]{1,0:T(8,128)(2,1)}, u32[]{:S(2)}) copy-start(bf16[512,1024]{1,0:T(8,128)(2,1)} %param.11) | copy-start | bytes 3145732
  19.4 1.3 copy-start.6
  28.3 37.2 %copy-start.7 = (u32[32]{0:T(128)S(1)}, u32[32]{0:T(128)}, u32[]{:S(2)}) copy-start(u32[32]{0:T(128)} %constant.58) | copy-start | bytes 388
  64.7 0.8 copy-start.1
  97.3 4.3 %copy-start.2 = (bf16[64,8,8,128]{3,2,1,0:T(8,128)(2,1)}, bf16[64,8,8,128]{3,2,1,0:T(8,128)(2,1)S(1)}, u32[]{:S(2)}) copy-start(bf16[64,8,8,128]{3,2,1,0:T(8,128)(2,1)S(1)} %copy.61) | copy-start | bytes 3145732
  160.6 1.6 copy-start.4
Sparse Core Ops, SparseCore 0:
  65.7 74.7 all-gather.3
where the time goes:
time: 174 us; the launch traced here: 171 us
  other arithmetic  53.9 us (31%)
  waiting for transfers between devices  32.8 us (19%)
  matrix products  31 us (18%)
  blocking collectives  26.4 us (15%)
  between operations  14.3 us (8%)
  local copies, waits for them, and re-layouts  12.3 us (7%)
    all_gather x1, waiting for transfers between devices, prefix(): gathered = jax.tree.map(lambda a: lax.all_gather(a, axis), part)  32.8 us
    unnamed x1, blocking collectives  26.4 us
    add x13, other arithmetic, combine_states(): second_state + second_decay[:, None, None] * first_state  15.5 us
    add x8, other arithmetic, carry_block(): state_in * decay_now[:, None, None] + block_term  14.3 us
    dynamic_update_slice x8, other arithmetic, body(): lax.scan(carry_block, (start_state, start_factor), (block_terms, block_de...  11.8 us
    dot_general x1, matrix products, body(): jnp.einsum('bihd,bihe->bhde', scaled, value_rows.astype(jnp.float32), pre...  7.52 us
    dot_general x3, matrix products, project(): jnp.dot(hidden, weight, preferred_element_type=jnp.float32)  7.1 us
    another operation x1, other arithmetic, body(): jnp.cumsum(decay_log.reshape(blocks, BLOCK, HEAD_COUNT), axis=1)  6.33 us
  transfers between devices with their start and end apart: 1, of which 1 were waited for; matrix products, arithmetic and copies ran while one was open for 9% of the time, Pallas kernels for 0%

commit v1 on v0

v1 whole, which is shorter than its diff:
```python
import functools

import jax
import jax.numpy as jnp
from jax import lax
from jax.experimental import pallas as pl
from jax.experimental.pallas import tpu as pltpu
from jax.sharding import PartitionSpec as P

D = 1024
HEAD_COUNT = 8
HEAD = 128
BLOCK = 64
PAIRS = HEAD_COUNT // 2
WIDE = 2 * HEAD
SPLIT = 1
ROWS = HEAD // SPLIT
CHUNKS = PAIRS * SPLIT
F32 = jnp.float32
BF16 = jnp.bfloat16
MESH = pl.DeviceIdType.MESH
RESET = -128.0


def dot(a, b):
    return jnp.dot(a, b, preferred_element_type=F32)


def kernel(outer, inner, tok, hidden_hbm, wq_hbm, wk_hbm, wv_hbm, wo_hbm, decay_hbm, docs_ref, out_ref,
           hid, wq, wk, wv, wo, dec, cum_s, cumt_s, q_s, k_s, v_s, qg_s, att_s, acc_s, w_s, grow_s,
           own, other, zin, zout, yin, yout, mout, sin, gbuf, fac,
           load_sem, g_send, g_recv, m1_send, m1_recv, z_send, z_recv, y_send, y_recv, m4_send, m4_recv):
    me = lax.axis_index("ctx")
    group = lax.axis_index("groups")
    core = lax.rem(me, 2)
    b = lax.rem(me // 2, inner)
    a = me // (2 * inner)
    slot = b * 2 + core
    plane = 2 * inner

    def at(aa, bb, cc):
        return (group, (aa * inner + bb) * 2 + cc)

    def peer(o):
        return lax.rem(slot + o, plane)

    loads = []

    def load(src, dst):
        c = pltpu.make_async_copy(src, dst, load_sem.at[len(loads)])
        c.start()
        loads.append(c)
        return c

    barrier = pltpu.get_barrier_semaphore()
    for o in range(1, plane):
        pl.semaphore_signal(barrier, inc=1, device_id=(group, a * plane + peer(o)), device_id_type=MESH)

    @pl.when(a > 0)
    def _():
        pl.semaphore_signal(barrier, inc=1, device_id=at(a - 1, b, core), device_id_type=MESH)

    @pl.when(a < outer - 1)
    def _():
        pl.semaphore_signal(barrier, inc=1, device_id=at(a + 1, b, core), device_id_type=MESH)

    ld_dec = load(decay_hbm, dec)
    ld_hid = load(hidden_hbm, hid)
    ld_kv = []
    for p in range(PAIRS):
        cols = pl.ds(p * WIDE, WIDE)
        ld_kv.append((load(wk_hbm.at[:, cols], wk.at[p]), load(wv_hbm.at[:, cols], wv.at[p])))
    ld_q = load(wq_hbm, wq)
    ld_o = load(wo_hbm, wo)

    row = lax.broadcasted_iota(jnp.int32, (tok, tok), 0)
    col = lax.broadcasted_iota(jnp.int32, (tok, tok), 1)
    lower = jnp.where(row >= col, 1.0, 0.0).astype(BF16)
    place = me * tok + lax.broadcasted_iota(jnp.int32, (tok, HEAD_COUNT), 0)
    hit = place == docs_ref[0]
    for i in range(1, docs_ref.shape[0]):
        hit = hit | (place == docs_ref[i])
    ld_dec.wait()
    cum_s[...] = jnp.zeros_like(cum_s)
    cum_s[:, 0:HEAD_COUNT] = dec[...] + jnp.where(hit, RESET, 0.0)
    full = cum_s[...]
    hi = full.astype(BF16)
    rest = full - hi.astype(F32)
    mid = rest.astype(BF16)
    low = (rest - mid.astype(F32)).astype(BF16)
    cum = dot(lower, hi) + (dot(lower, mid) + dot(lower, low))
    cum_s[...] = cum
    cumt = cum.T
    cumt_s[...] = cumt[0:HEAD_COUNT, :]
    w_s[...] = jnp.exp(cum[tok - 1:tok, :] - cum)
    grow_s[...] = jnp.exp(cum)
    gown = jnp.exp(jnp.broadcast_to(cumt[0:HEAD_COUNT, tok - 1:tok], (HEAD_COUNT, HEAD)))
    gbuf[pl.ds(slot, 1)] = gown[None]

    pl.semaphore_wait(barrier, plane - 1 + jnp.where(a > 0, 1, 0) + jnp.where(a < outer - 1, 1, 0))

    def g_copy(o):
        return pltpu.make_async_remote_copy(
            src_ref=gbuf.at[slot], dst_ref=gbuf.at[slot], send_sem=g_send.at[o], recv_sem=g_recv.at[slot],
            device_id=(group, a * plane + peer(o)), device_id_type=MESH)

    def g_land(o):
        s = peer(o)
        return pltpu.make_async_remote_copy(
            src_ref=gbuf.at[s], dst_ref=gbuf.at[s], send_sem=g_send.at[o], recv_sem=g_recv.at[s],
            device_id=(group, a * plane + peer(o)), device_id_type=MESH)

    for o in range(1, plane):
        g_copy(o).start()

    @pl.when(a == 0)
    def _():
        zin[...] = jnp.zeros_like(zin)
        for o in range(1, inner):
            bb = lax.rem(b + o, inner)

            @pl.when(bb > b)
            def _():
                for qq in range(CHUNKS):
                    yin[qq, pl.ds(bb, 1)] = jnp.zeros((1, ROWS, HEAD), F32)

    def head_of(p, c):
        return 2 * p + c

    def m1_copy(q):
        p, s = divmod(q, SPLIT)
        return pltpu.make_async_remote_copy(
            src_ref=own.at[head_of(p, 1 - core) * SPLIT + s], dst_ref=other.at[q],
            send_sem=m1_send.at[q], recv_sem=m1_recv.at[q], device_id=at(a, b, 1 - core), device_id_type=MESH)

    def z_copy(q):
        return pltpu.make_async_remote_copy(
            src_ref=zout.at[q], dst_ref=zin.at[q], send_sem=z_send.at[q], recv_sem=z_recv.at[q],
            device_id=at(jnp.minimum(a + 1, outer - 1), b, core), device_id_type=MESH)

    def y_copy(q, o, src):
        return pltpu.make_async_remote_copy(
            src_ref=src.at[q], dst_ref=yin.at[q, b], send_sem=y_send.at[q, o], recv_sem=y_recv.at[q, b],
            device_id=at(a, lax.rem(b + o, inner), core), device_id_type=MESH)

    def y_land(q, o):
        bb = lax.rem(b + o, inner)
        return pltpu.make_async_remote_copy(
            src_ref=yout.at[q], dst_ref=yin.at[q, bb], send_sem=y_send.at[q, o], recv_sem=y_recv.at[q, bb],
            device_id=at(a, bb, core), device_id_type=MESH)

    def m4_copy(q, c):
        p, s = divmod(q, SPLIT)
        return pltpu.make_async_remote_copy(
            src_ref=mout.at[q], dst_ref=sin.at[head_of(p, c) * SPLIT + s],
            send_sem=m4_send.at[q], recv_sem=m4_recv.at[q], device_id=at(a, b, 1 - core), device_id_type=MESH)

    def factor(k, q):
        return fac[k, pl.ds(head_of(q // SPLIT, core), 1), :]

    def mine(q):
        p, s = divmod(q, SPLIT)
        return own[head_of(p, core) * SPLIT + s]

    def factors():
        for o in range(1, plane):
            g_land(o).wait_recv()
        chip = [gbuf[2 * i] * gbuf[2 * i + 1] for i in range(inner)]
        one = jnp.ones_like(chip[0])
        every, post, pre, upto = one, one, one, one
        for i in range(inner):
            every = every * chip[i]
            post = post * jnp.where(i > b, chip[i], one)
            pre = pre * jnp.where(i < b, chip[i], one)
            upto = upto * jnp.where(i <= b, chip[i], one)
        fac[0], fac[1], fac[2], fac[3] = every, post, upto, pre
        fac[4] = gbuf[pl.ds(2 * b, 1)][0]
        fac[5] = gbuf[pl.ds(2 * b + 1, 1)][0]
        for j in range(inner):
            between = one
            for i in range(j + 1, inner):
                between = between * jnp.where(i < b, chip[i], one)
            fac[6 + j] = jnp.where(j < b, between, pre)

    def relay(q):
        m1_copy(q).wait_recv()

        @pl.when(a > 0)
        def _():
            z_copy(q).wait_recv()

        mn, ot, before = mine(q), other[q], zin[q]
        first = jnp.where(core == 0, mn, ot)
        second = jnp.where(core == 0, ot, mn)
        total = factor(5, q) * first + second
        zout[q] = factor(0, q) * before + factor(1, q) * total
        yout[q] = factor(2, q) * before + total

        @pl.when(a < outer - 1)
        def _():
            z_copy(q).start()

        for o in range(1, inner):
            bb = lax.rem(b + o, inner)

            @pl.when(bb > b)
            def _():
                y_copy(q, o, yout).start()

            @pl.when((bb < b) & (a > 0))
            def _():
                y_copy(q, o, zin).start()

    def merge(q):
        state = factor(3, q) * zin[q]
        for o in range(1, inner):
            bb = lax.rem(b + o, inner)

            @pl.when((bb < b) | (a > 0))
            def _():
                y_land(q, o).wait_recv()

            weight = fac[pl.ds(6 + bb, 1), pl.ds(head_of(q // SPLIT, core), 1), :][0]
            state = state + weight * yin[q, pl.ds(bb, 1)][0]
        first = jnp.where(core == 0, mine(q), other[q])
        late = factor(4, q) * state + first
        p, s = divmod(q, SPLIT)
        sin[pl.ds(head_of(p, core) * SPLIT + s, 1)] = jnp.where(core == 0, state, late)[None]
        mout[q] = jnp.where(core == 0, late, state)
        m4_copy(q, core).start()

    def keys_values(p):
        ld_kv[p][0].wait()
        kp = dot(hid[...], wk[p]).astype(BF16)
        k_s[p] = kp
        ld_kv[p][1].wait()
        vp = dot(hid[...], wv[p]).astype(BF16)
        v_s[p] = vp
        scale = jnp.concatenate(
            [jnp.broadcast_to(w_s[:, 2 * p + i:2 * p + i + 1], (tok, HEAD)) for i in range(2)], axis=1)
        scaled = (kp.astype(F32) * scale).astype(BF16)
        both = lax.dot_general(scaled, vp, (((0,), (0,)), ((), ())), preferred_element_type=F32)
        for i in range(2):
            for s in range(SPLIT):
                own[(2 * p + i) * SPLIT + s] = both[i * HEAD + s * ROWS:i * HEAD + (s + 1) * ROWS,
                                                    i * HEAD:(i + 1) * HEAD]
        for s in range(SPLIT):
            m1_copy(p * SPLIT + s).start()

    def query(p):
        qp = dot(hid[...], wq[:, p * WIDE:(p + 1) * WIDE]).astype(BF16)
        q_s[p] = qp
        scale = jnp.concatenate(
            [jnp.broadcast_to(grow_s[:, 2 * p + i:2 * p + i + 1], (tok, HEAD)) for i in range(2)], axis=1)
        qg_s[p] = (qp.astype(F32) * scale).astype(BF16)

    half = tok // 2
    tri = (lax.broadcasted_iota(jnp.int32, (half, half), 0) >= lax.broadcasted_iota(jnp.int32, (half, half), 1))

    def inside(h):
        p, i = divmod(h, 2)
        lanes = slice(i * HEAD, (i + 1) * HEAD)
        for r in range(2):
            rows = slice(r * half, (r + 1) * half)
            qh = q_s[p, rows, lanes]
            cj = cum_s[rows, h:h + 1]
            total = None
            for c in range(r + 1):
                cols = slice(c * half, (c + 1) * half)
                score = lax.dot_general(qh, k_s[p, cols, lanes], (((1,), (1,)), ((), ())),
                                        preferred_element_type=F32)
                fade = jnp.exp(cj - cumt_s[h:h + 1, cols])
                if c == r:
                    fade = jnp.where(tri, fade, 0.0)
                part = dot((fade * score).astype(BF16), v_s[p, cols, lanes])
                total = part if total is None else total + part
            att_s[rows, h * HEAD:(h + 1) * HEAD] = total

    def finish(p):
        for s in range(SPLIT):
            m4_copy(p * SPLIT + s, 1 - core).wait_recv()
        halves = []
        for i in range(2):
            h = 2 * p + i
            lanes = slice(i * HEAD, (i + 1) * HEAD)
            state = jnp.concatenate([sin[h * SPLIT + s] for s in range(SPLIT)], axis=0) if SPLIT > 1 else sin[h]
            att = att_s[:, h * HEAD:(h + 1) * HEAD] + dot(qg_s[p, :, lanes], state.astype(BF16))
            norm = lax.rsqrt(jnp.mean(att * att, axis=1, keepdims=True) + 1e-06)
            halves.append((att * norm).astype(BF16))
        normed = jnp.concatenate(halves, axis=1)
        part = dot(normed, wo[p * WIDE:(p + 1) * WIDE, :])
        if p == 0:
            acc_s[...] = part
        elif p < PAIRS - 1:
            acc_s[...] += part
        else:
            out_ref[...] = (acc_s[...] + part).astype(BF16)

    ld_hid.wait()
    for p in range(PAIRS):
        keys_values(p)
        if p == 0:
            factors()
        else:
            @pl.when(a == 0)
            def _():
                for s in range(SPLIT):
                    relay((p - 1) * SPLIT + s)
    ld_q.wait()
    work = [functools.partial(query, p) for p in range(PAIRS)] + [functools.partial(inside, h) for h in range(HEAD_COUNT)]
    plan = {(0, PAIRS - 1): 0, (1, 0): 2, (1, 1): 5, (1, 2): 8, (2, 0): 8}
    for u, unit in enumerate(work):
        unit()
        for (aa, p), when in plan.items():
            if when == u:
                @pl.when(a == aa)
                def _():
                    for s in range(SPLIT):
                        relay(p * SPLIT + s)

    def late_relay(p):
        early = [aa for (aa, pp) in plan if pp == p] + [0]
        cond = a > max(early)

        @pl.when(cond)
        def _():
            for s in range(SPLIT):
                relay(p * SPLIT + s)

    def merges(p):
        for s in range(SPLIT):
            merge(p * SPLIT + s)

    ld_o.wait()
    late_relay(0)
    late_relay(1)
    merges(0)
    late_relay(2)
    merges(1)
    finish(0)
    late_relay(3)
    merges(2)
    finish(1)
    merges(3)
    finish(2)
    finish(3)

    for o in range(1, plane):
        g_copy(o).wait_send()
    for q in range(CHUNKS):
        m1_copy(q).wait_send()
        m4_copy(q, core).wait_send()

        @pl.when(a < outer - 1)
        def _():
            z_copy(q).wait_send()

        for o in range(1, inner):
            bb = lax.rem(b + o, inner)

            @pl.when((bb > b) | (a > 0))
            def _():
                y_copy(q, o, yout).wait_send()


def body(outer, inner, hidden, query_weight, key_weight, value_weight, output_weight, decay_log, doc_starts):
    tok = hidden.shape[0]
    plane = 2 * inner
    state = (ROWS, HEAD)
    scratch = [
        pltpu.VMEM((tok, D), BF16),
        pltpu.VMEM((D, D), BF16),
        pltpu.VMEM((PAIRS, D, WIDE), BF16),
        pltpu.VMEM((PAIRS, D, WIDE), BF16),
        pltpu.VMEM((D, D), BF16),
        pltpu.VMEM((tok, HEAD_COUNT), F32),
        pltpu.VMEM((tok, HEAD), F32),
        pltpu.VMEM((HEAD_COUNT, tok), F32),
        pltpu.VMEM((PAIRS, tok, WIDE), BF16),
        pltpu.VMEM((PAIRS, tok, WIDE), BF16),
        pltpu.VMEM((PAIRS, tok, WIDE), BF16),
        pltpu.VMEM((PAIRS, tok, WIDE), BF16),
        pltpu.VMEM((tok, D), F32),
        pltpu.VMEM((tok, D), F32),
        pltpu.VMEM((tok, HEAD), F32),
        pltpu.VMEM((tok, HEAD), F32),
        pltpu.VMEM((HEAD_COUNT * SPLIT,) + state, F32),
        pltpu.VMEM((CHUNKS,) + state, F32),
        pltpu.VMEM((CHUNKS,) + state, F32),
        pltpu.VMEM((CHUNKS,) + state, F32),
        pltpu.VMEM((CHUNKS, inner) + state, F32),
        pltpu.VMEM((CHUNKS,) + state, F32),
        pltpu.VMEM((CHUNKS,) + state, F32),
        pltpu.VMEM((HEAD_COUNT * SPLIT,) + state, F32),
        pltpu.VMEM((plane, HEAD_COUNT, HEAD), F32),
        pltpu.VMEM((6 + inner, HEAD_COUNT, HEAD), F32),
        pltpu.SemaphoreType.DMA((4 + 2 * PAIRS,)),
        pltpu.SemaphoreType.DMA((plane,)),
        pltpu.SemaphoreType.DMA((plane,)),
        pltpu.SemaphoreType.DMA((CHUNKS,)),
        pltpu.SemaphoreType.DMA((CHUNKS,)),
        pltpu.SemaphoreType.DMA((CHUNKS,)),
        pltpu.SemaphoreType.DMA((CHUNKS,)),
        pltpu.SemaphoreType.DMA((CHUNKS, inner)),
        pltpu.SemaphoreType.DMA((CHUNKS, inner)),
        pltpu.SemaphoreType.DMA((CHUNKS,)),
        pltpu.SemaphoreType.DMA((CHUNKS,)),
    ]
    hbm = pl.BlockSpec(memory_space=pl.ANY)
    return pl.pallas_call(
        functools.partial(kernel, outer, inner, tok),
        out_shape=jax.ShapeDtypeStruct((tok, D), BF16),
        in_specs=[hbm] * 6 + [pl.BlockSpec(memory_space=pltpu.SMEM)],
        out_specs=pl.BlockSpec(memory_space=pltpu.VMEM),
        scratch_shapes=scratch,
        compiler_params=pltpu.CompilerParams(collective_id=0, has_side_effects=True,
                                             vmem_limit_bytes=50 * 1024 * 1024),
        name="decayed_layer",
    )(hidden, query_weight, key_weight, value_weight, output_weight, decay_log, doc_starts)


def solution(mesh):
    chips = mesh.shape["ctx"] // 2
    inner = 1
    while inner * inner * 4 <= chips:
        inner *= 2
    inner = max(inner, 1)
    outer = chips // inner
    spread = P(("groups", "ctx"), None)
    in_specs = (spread, P(), P(), P(), P(), spread, P("groups"))
    return jax.shard_map(functools.partial(body, outer, inner), mesh=mesh, in_specs=in_specs,
                         out_specs=spread, check_vma=False)
```

time: 174 us -> 32.8 us (0.19); the launches traced: 171 us -> 32.6 us
  other arithmetic: 53.9 us -> 0 us
  waiting for transfers between devices: 32.8 us -> 0 us
  matrix products: 31 us -> 0 us
  Pallas kernels: 0 us -> 28.9 us
  blocking collectives: 26.4 us -> 0 us
  between operations: 14.3 us -> 0.03 us
  local copies, waits for them, and re-layouts: 12.3 us -> 3.69 us
    all_gather x1 -> x0, waiting for transfers between devices: 32.8 us -> none  [prefix(): gathered = jax.tree.map(lambda a: lax.all_gather(a, axis), part)]
    dot_general x8 -> x0, matrix products: 31 us -> none  [the longest x1 7.52 us: body(): jnp.einsum('bihd,bihe->bhde', scaled, value_rows.astype(jnp.float32), pre...]
    add x22 -> x0, other arithmetic: 29.7 us -> none  [the longest x13 15.5 us: combine_states(): second_state + second_decay[:, None, None] * first_state]
    pallas_call x0 -> x1, Pallas kernels: none -> 28.9 us  [body(): pl.pallas_call(functools.partial(kernel, outer, inner, tok), out_shape=ja...]
    unnamed x1 -> x0, blocking collectives: 26.4 us -> none
    dynamic_update_slice x8 -> x0, other arithmetic: 11.8 us -> none  [body(): lax.scan(carry_block, (start_state, start_factor), (block_terms, block_de...]
    another operation x1 -> x0, other arithmetic: 6.33 us -> none  [body(): jnp.cumsum(decay_log.reshape(blocks, BLOCK, HEAD_COUNT), axis=1)]
    mul x8 -> x0, other arithmetic: 5.1 us -> none  [carry_block(): factor_in * decay_now]
  transfers between devices with their start and end apart: 1 -> 0, of which waited for: 1 -> 0; matrix products, arithmetic and copies ran while one was open for 9% -> 0% of each run, Pallas kernels for 0% -> 0%
where the time goes in v1:
time: 32.8 us; the launch traced here: 32.6 us
  Pallas kernels  28.9 us (88%)
  local copies, waits for them, and re-layouts  3.69 us (11%)
    pallas_call x1, Pallas kernels, body(): pl.pallas_call(functools.partial(kernel, outer, inner, tok), out_shape=ja...  28.9 us
    unnamed x6, local copies, waits for them, and re-layouts  3.69 us

profile of v1, /device:TPU:27, one launch (start us, length us, event | category | flops | bytes accessed | tf_op | source)
XLA Modules:
  0.0 32.6 jit_solution(360239902682403647)
XLA Ops:
  0.0 0.8 %copy.8.decay_hbm = f32[512,8]{1,0:T(8,128)S(1)} copy(f32[512,8]{0,1:T(8,128)} %param.12) | data formatting | bytes 32768 | tf_op args[5]
  0.8 0.0 copy-start
  0.9 1.2 %copy-done = bf16[512,1024]{1,0:T(8,128)(2,1)S(1)} copy-done((bf16[512,1024]{1,0:T(8,128)(2,1)S(1)}, bf16[512,1024]{1,0:T(8,128)(2,1)}, u32[]{:S(2)}) %copy-start) | copy-done | bytes 1048600
  2.1 0.0 copy-start.1
  2.1 0.7 %copy-done.1 = s32[4]{0:T(128)S(1)} copy-done((s32[4]{0:T(128)S(1)}, s32[4]{0:T(128)}, u32[]{:S(2)}) %copy-start.1) | copy-done | bytes 40
  2.7 28.9 %decayed_layer.1 = bf16[512,1024]{1,0:T(8,128)(2,1)S(1)} custom-call(bf16[512,1024]{1,0:T(8,128)(2,1)S(1)} %copy-done, bf16[1024,1024]{1,0:T(8,128)(2,1)} %wq_hbm.1, bf16[1024,1024]{1,0:T(8,128)(2,1)} %wk_hbm.1, bf16[1024,1024]{1,0:T(8,128)(2,1)} %wv_hbm.1, bf16[1024,1024]{1,0:T(8,128)(2,1)} %wo_hbm.1, f32[512,8]{1,0:T(8,128)S(1)} %copy.8.decay_hbm, ...), custom_call_target="tpu_custom_call" | custom-call | tf_op jit(solution)/shard_map/decayed_layer/pallas_call | solution.py:410
  31.6 1.0 %copy.10 = bf16[512,1024]{1,0:T(8,128)(2,1)} copy(bf16[512,1024]{1,0:T(8,128)(2,1)S(1)} %decayed_layer.1) | data formatting | bytes 2097152
Async XLA Ops:
  0.8 1.2 %copy-start = (bf16[512,1024]{1,0:T(8,128)(2,1)S(1)}, bf16[512,1024]{1,0:T(8,128)(2,1)}, u32[]{:S(2)}) copy-start(bf16[512,1024]{1,0:T(8,128)(2,1)} %hidden_hbm.1) | copy-start | bytes 3145732
  2.1 0.7 %copy-start.1 = (s32[4]{0:T(128)S(1)}, s32[4]{0:T(128)}, u32[]{:S(2)}) copy-start(s32[4]{0:T(128)} %docs_ref.1) | copy-start | bytes 52

commit v2 on v1

--- a/solution.py
+++ b/solution.py
@@ -13,7 +13,7 @@
 BLOCK = 64
 PAIRS = HEAD_COUNT // 2
 WIDE = 2 * HEAD
-SPLIT = 1
+SPLIT = 2
 ROWS = HEAD // SPLIT
 CHUNKS = PAIRS * SPLIT
 F32 = jnp.float32
@@ -26,8 +26,8 @@
     return jnp.dot(a, b, preferred_element_type=F32)
 
 
-def kernel(outer, inner, tok, hidden_hbm, wq_hbm, wk_hbm, wv_hbm, wo_hbm, decay_hbm, docs_ref, out_ref,
-           hid, wq, wk, wv, wo, dec, cum_s, cumt_s, q_s, k_s, v_s, qg_s, att_s, acc_s, w_s, grow_s,
+def kernel(outer, inner, tok, hidden_hbm, wq_hbm, wk_hbm, wv_hbm, wo_hbm, decay_hbm, docs_hbm, out_ref,
+           hid, wq, wk, wv, wo, dec, docs, cum_s, cumt_s, q_s, k_s, v_s, qg_s, att_s, acc_s, w_s, grow_s,
            own, other, zin, zout, yin, yout, mout, sin, gbuf, fac,
            load_sem, g_send, g_recv, m1_send, m1_recv, z_send, z_recv, y_send, y_recv, m4_send, m4_recv):
     me = lax.axis_index("ctx")
@@ -64,6 +64,7 @@
     def _():
         pl.semaphore_signal(barrier, inc=1, device_id=at(a + 1, b, core), device_id_type=MESH)
 
+    ld_docs = load(docs_hbm, docs)
     ld_dec = load(decay_hbm, dec)
     ld_hid = load(hidden_hbm, hid)
     ld_kv = []
@@ -75,29 +76,27 @@
 
     row = lax.broadcasted_iota(jnp.int32, (tok, tok), 0)
     col = lax.broadcasted_iota(jnp.int32, (tok, tok), 1)
-    lower = jnp.where(row >= col, 1.0, 0.0).astype(BF16)
-    place = me * tok + lax.broadcasted_iota(jnp.int32, (tok, HEAD_COUNT), 0)
-    hit = place == docs_ref[0]
-    for i in range(1, docs_ref.shape[0]):
-        hit = hit | (place == docs_ref[i])
+    upper = jnp.where(row <= col, 1.0, 0.0).astype(BF16)
+    place = me * tok + lax.broadcasted_iota(jnp.int32, (HEAD_COUNT, tok), 1)
+    ld_docs.wait()
+    hit = place == docs[0]
+    for i in range(1, docs.shape[0]):
+        hit = hit | (place == docs[i])
     ld_dec.wait()
-    cum_s[...] = jnp.zeros_like(cum_s)
-    cum_s[:, 0:HEAD_COUNT] = dec[...] + jnp.where(hit, RESET, 0.0)
-    full = cum_s[...]
-    hi = full.astype(BF16)
-    rest = full - hi.astype(F32)
-    mid = rest.astype(BF16)
-    low = (rest - mid.astype(F32)).astype(BF16)
-    cum = dot(lower, hi) + (dot(lower, mid) + dot(lower, low))
+    full = dec[...] + jnp.where(hit, RESET, 0.0)
+    hi = full.astype(BF16).astype(F32)
+    rest = full - hi
+    mid = rest.astype(BF16).astype(F32)
+    parts = dot(jnp.concatenate([hi, mid, rest - mid], axis=0).astype(BF16), upper)
+    n = HEAD_COUNT
+    cumt = parts[0:n] + (parts[n:2 * n] + parts[2 * n:3 * n])
+    cumt_s[...] = cumt
+    cum = jnp.concatenate([cumt, jnp.zeros((HEAD - n, tok), F32)], axis=0).T
     cum_s[...] = cum
-    cumt = cum.T
-    cumt_s[...] = cumt[0:HEAD_COUNT, :]
     w_s[...] = jnp.exp(cum[tok - 1:tok, :] - cum)
     grow_s[...] = jnp.exp(cum)
-    gown = jnp.exp(jnp.broadcast_to(cumt[0:HEAD_COUNT, tok - 1:tok], (HEAD_COUNT, HEAD)))
+    gown = jnp.exp(jnp.broadcast_to(cumt[:, tok - 1:tok], (HEAD_COUNT, HEAD)))
     gbuf[pl.ds(slot, 1)] = gown[None]
-
-    pl.semaphore_wait(barrier, plane - 1 + jnp.where(a > 0, 1, 0) + jnp.where(a < outer - 1, 1, 0))
 
     def g_copy(o):
         return pltpu.make_async_remote_copy(
@@ -109,9 +108,6 @@
         return pltpu.make_async_remote_copy(
             src_ref=gbuf.at[s], dst_ref=gbuf.at[s], send_sem=g_send.at[o], recv_sem=g_recv.at[s],
             device_id=(group, a * plane + peer(o)), device_id_type=MESH)
-
-    for o in range(1, plane):
-        g_copy(o).start()
 
     @pl.when(a == 0)
     def _():
@@ -229,6 +225,11 @@
         mout[q] = jnp.where(core == 0, late, state)
         m4_copy(q, core).start()
 
+    def greet():
+        pl.semaphore_wait(barrier, plane - 1 + jnp.where(a > 0, 1, 0) + jnp.where(a < outer - 1, 1, 0))
+        for o in range(1, plane):
+            g_copy(o).start()
+
     def keys_values(p):
         ld_kv[p][0].wait()
         kp = dot(hid[...], wk[p]).astype(BF16)
@@ -244,6 +245,8 @@
             for s in range(SPLIT):
                 own[(2 * p + i) * SPLIT + s] = both[i * HEAD + s * ROWS:i * HEAD + (s + 1) * ROWS,
                                                     i * HEAD:(i + 1) * HEAD]
+        if p == 0:
+            greet()
         for s in range(SPLIT):
             m1_copy(p * SPLIT + s).start()
 
@@ -299,16 +302,16 @@
     ld_hid.wait()
     for p in range(PAIRS):
         keys_values(p)
-        if p == 0:
+        if p == 1:
             factors()
-        else:
+        if p > 0:
             @pl.when(a == 0)
             def _():
                 for s in range(SPLIT):
                     relay((p - 1) * SPLIT + s)
     ld_q.wait()
     work = [functools.partial(query, p) for p in range(PAIRS)] + [functools.partial(inside, h) for h in range(HEAD_COUNT)]
-    plan = {(0, PAIRS - 1): 0, (1, 0): 2, (1, 1): 5, (1, 2): 8, (2, 0): 8}
+    plan = {(0, 3): 0, (1, 0): 0, (1, 1): 2, (1, 2): 5, (1, 3): 6, (2, 0): 6, (2, 1): 8, (2, 2): 10, (2, 3): 11}
     for u, unit in enumerate(work):
         unit()
         for (aa, p), when in plan.items():
@@ -373,7 +376,8 @@
         pltpu.VMEM((PAIRS, D, WIDE), BF16),
         pltpu.VMEM((PAIRS, D, WIDE), BF16),
         pltpu.VMEM((D, D), BF16),
-        pltpu.VMEM((tok, HEAD_COUNT), F32),
+        pltpu.VMEM((HEAD_COUNT, tok), F32),
+        pltpu.SMEM(doc_starts.shape, jnp.int32),
         pltpu.VMEM((tok, HEAD), F32),
         pltpu.VMEM((HEAD_COUNT, tok), F32),
         pltpu.VMEM((PAIRS, tok, WIDE), BF16),
@@ -394,7 +398,7 @@
         pltpu.VMEM((HEAD_COUNT * SPLIT,) + state, F32),
         pltpu.VMEM((plane, HEAD_COUNT, HEAD), F32),
         pltpu.VMEM((6 + inner, HEAD_COUNT, HEAD), F32),
-        pltpu.SemaphoreType.DMA((4 + 2 * PAIRS,)),
+        pltpu.SemaphoreType.DMA((5 + 2 * PAIRS,)),
         pltpu.SemaphoreType.DMA((plane,)),
         pltpu.SemaphoreType.DMA((plane,)),
         pltpu.SemaphoreType.DMA((CHUNKS,)),
@@ -406,17 +410,17 @@
         pltpu.SemaphoreType.DMA((CHUNKS,)),
         pltpu.SemaphoreType.DMA((CHUNKS,)),
     ]
-    hbm = pl.BlockSpec(memory_space=pl.ANY)
+    hbm = pl.BlockSpec(memory_space=pltpu.HBM)
     return pl.pallas_call(
         functools.partial(kernel, outer, inner, tok),
         out_shape=jax.ShapeDtypeStruct((tok, D), BF16),
-        in_specs=[hbm] * 6 + [pl.BlockSpec(memory_space=pltpu.SMEM)],
+        in_specs=[hbm] * 7,
         out_specs=pl.BlockSpec(memory_space=pltpu.VMEM),
         scratch_shapes=scratch,
         compiler_params=pltpu.CompilerParams(collective_id=0, has_side_effects=True,
-                                             vmem_limit_bytes=50 * 1024 * 1024),
+                                             vmem_limit_bytes=63 * 1024 * 1024),
         name="decayed_layer",
-    )(hidden, query_weight, key_weight, value_weight, output_weight, decay_log, doc_starts)
+    )(hidden, query_weight, key_weight, value_weight, output_weight, decay_log.T, doc_starts)
 
 
 def solution(mesh):

time: 32.8 us -> 30.8 us (0.939)
  local copies, waits for them, and re-layouts: 3.69 us -> 2.26 us
  Pallas kernels: 28.9 us -> 28.4 us
    unnamed x6 -> x1, local copies, waits for them, and re-layouts: 3.69 us -> 2.26 us
    pallas_call x1, Pallas kernels: 28.9 us -> 28.4 us  [body(): pl.pallas_call(functools.partial(kernel, outer, inner, tok), out_shape=ja...]
where the time goes in v2:
time: 30.8 us; the launch traced here: 30.7 us
  Pallas kernels  28.4 us (92%)
  local copies, waits for them, and re-layouts  2.26 us (7%)
    pallas_call x1, Pallas kernels, body(): pl.pallas_call(functools.partial(kernel, outer, inner, tok), out_shape=ja...  28.4 us
    unnamed x1, local copies, waits for them, and re-layouts  2.26 us

profile of v2, /device:TPU:27, one launch (start us, length us, event | category | flops | bytes accessed | tf_op | source)
XLA Modules:
  0.0 30.7 jit_solution(15095028942966470687)
XLA Ops:
  0.0 28.4 %decayed_layer.1 = bf16[512,1024]{1,0:T(8,128)(2,1)} custom-call(bf16[512,1024]{1,0:T(8,128)(2,1)} %hidden_hbm.1, bf16[1024,1024]{1,0:T(8,128)(2,1)} %wq_hbm.1, bf16[1024,1024]{1,0:T(8,128)(2,1)} %wk_hbm.1, bf16[1024,1024]{1,0:T(8,128)(2,1)} %wv_hbm.1, bf16[1024,1024]{1,0:T(8,128)(2,1)} %wo_hbm.1, f32[8,512]{1,0:T(8,128)} %bitcast.1, s32[4]{0:T(128)} %docs_hbm.1), custom_call_target="tpu_custom_call" | custom-call | tf_op jit(solution)/shard_map/decayed_layer/pallas_call | solution.py:414
  28.4 2.3 %copy.9 = bf16[512,1024]{1,0:T(8,128)(2,1)} copy(bf16[512,1024]{1,0:T(8,128)(2,1)} %decayed_layer.1) | data formatting | bytes 2097152

commit v3 on v2

--- a/solution.py
+++ b/solution.py
@@ -418,7 +418,7 @@
         out_specs=pl.BlockSpec(memory_space=pltpu.VMEM),
         scratch_shapes=scratch,
         compiler_params=pltpu.CompilerParams(collective_id=0, has_side_effects=True,
-                                             vmem_limit_bytes=63 * 1024 * 1024),
+                                             vmem_limit_bytes=52 * 1024 * 1024),
         name="decayed_layer",
     )(hidden, query_weight, key_weight, value_weight, output_weight, decay_log.T, doc_starts)
 

time: 30.8 us -> 30 us (0.974)
  Pallas kernels: 28.4 us -> 27.4 us
    pallas_call x1, Pallas kernels: 28.4 us -> 27.4 us  [body(): pl.pallas_call(functools.partial(kernel, outer, inner, tok), out_shape=ja...]
    unnamed x1 -> x5, local copies, waits for them, and re-layouts: 2.26 us -> 2.34 us
where the time goes in v3:
time: 30 us; the launch traced here: 29.8 us
  Pallas kernels  27.4 us (91%)
  local copies, waits for them, and re-layouts  2.34 us (8%)
    pallas_call x1, Pallas kernels, body(): pl.pallas_call(functools.partial(kernel, outer, inner, tok), out_shape=ja...  27.4 us
    unnamed x5, local copies, waits for them, and re-layouts  2.34 us

profile of v3, /device:TPU:27, one launch (start us, length us, event | category | flops | bytes accessed | tf_op | source)
XLA Modules:
  0.0 29.8 jit_solution(8505563262845590106)
XLA Ops:
  0.0 0.0 copy-start
  0.0 0.7 %copy-done = f32[512,8]{0,1:T(8,128)S(1)} copy-done((f32[512,8]{0,1:T(8,128)S(1)}, f32[512,8]{0,1:T(8,128)}, u32[]{:S(2)}) %copy-start) | copy-done | bytes 16408
  0.7 0.0 copy-start.1
  0.7 0.7 %copy-done.1 = s32[4]{0:T(128)S(1)} copy-done((s32[4]{0:T(128)S(1)}, s32[4]{0:T(128)}, u32[]{:S(2)}) %copy-start.1) | copy-done | bytes 40
  1.4 27.4 %decayed_layer.1 = bf16[512,1024]{1,0:T(8,128)(2,1)S(1)} custom-call(bf16[512,1024]{1,0:T(8,128)(2,1)} %hidden_hbm.1, bf16[1024,1024]{1,0:T(8,128)(2,1)} %wq_hbm.1, bf16[1024,1024]{1,0:T(8,128)(2,1)} %wk_hbm.1, bf16[1024,1024]{1,0:T(8,128)(2,1)} %wv_hbm.1, bf16[1024,1024]{1,0:T(8,128)(2,1)} %wo_hbm.1, f32[8,512]{1,0:T(8,128)S(1)} %bitcast.1, s32[4]{0:T(128)S(1)} %copy-done.1), custom_call_target="tpu_custom_call" | custom-call | tf_op jit(solution)/shard_map/decayed_layer/pallas_call | solution.py:414
  28.8 1.0 %copy.9 = bf16[512,1024]{1,0:T(8,128)(2,1)} copy(bf16[512,1024]{1,0:T(8,128)(2,1)S(1)} %decayed_layer.1) | data formatting | bytes 2097152
Async XLA Ops:
  0.0 0.7 %copy-start = (f32[512,8]{0,1:T(8,128)S(1)}, f32[512,8]{0,1:T(8,128)}, u32[]{:S(2)}) copy-start(f32[512,8]{0,1:T(8,128)} %param.12) | copy-start | bytes 49156
  0.7 0.7 %copy-start.1 = (s32[4]{0:T(128)S(1)}, s32[4]{0:T(128)}, u32[]{:S(2)}) copy-start(s32[4]{0:T(128)} %docs_hbm.1) | copy-start | bytes 52
